TPU v7x, 32 devices: a whole 2x2x4 slice. The times are simulated.
32 devices in a mesh: gx: 8 (over z, y), gy: 4 (over x, core).
Axes of the slice: x: 2, y: 2, z: 4, core: 2. Of those that a mesh axis runs over, the one named last changes fastest.
Arguments:
- anomalies: float32 [16384, 1024], P(('gx', 'gy')), may hold values from -50 to 50
- obs_rows: int32 [8, 256], replicated, may hold values from 0 to 6143
- obs_var: float32 [8, 256], P('gx'), may hold values from 0.5 to 20
- taper_level: int32 [8, 3, 4], replicated, may hold values from 0 to 3
Outputs:
- posterior: float32 [16384, 1024], P(('gx', 'gy'))
All inputs are finite; a program needn't handle non-finite values.
Results may differ from a plain program's by a relative error of at most 0.035.
The roundings to bfloat16 on the way count: a program that leaves them out, or rounds other values in their place, can miss the bound.
Values may be sent and summed in bfloat16 or wider, within the bound.
A program may use at most 64 MiB of HBM per device.

v0:
```python
import jax
import jax.numpy as jnp
from jax import lax
from jax.experimental import pallas as pl
from jax.experimental.pallas import tpu as pltpu
from jax.sharding import PartitionSpec as P

NCOL = 4
NS_STEPS = 12
SLOTS = 3
WINDOW = 8
CHUNK = 256
PIECES = 2
MESH = pl.DeviceIdType.MESH
BF16 = jnp.bfloat16
F32 = jnp.float32


class Gather:
    def __init__(self, part, var, blocks, varies, buffers, sems):
        self.part, self.var, self.blocks, self.varies = part, var, blocks, varies
        self.rec1, self.acc1, self.rec2, self.acc2, self.rec3 = buffers
        (self.s1, self.r1, self.s2, self.r2, self.s3, self.r3, self.zs, self.zr, self.ys, self.yr,
         self.xs, self.xr, self.cs, self.cr, self.vs, self.vr) = sems
        i, j = lax.axis_index("gx"), lax.axis_index("gy")
        self.i, self.j = i, j
        self.z, self.y, self.x, self.core = i // 2, i % 2, j // 2, j % 2
        self.cpart = (i, j + 1 - 2 * self.core)
        self.xpart = (i, j + 2 - 4 * self.x)
        self.ypart = (i + 1 - 2 * self.y, j)
        self.quarter = blocks.shape[4]

    def remote(self, src, dst, send, recv, who):
        return pltpu.make_async_remote_copy(
            src_ref=src, dst_ref=dst, send_sem=send, recv_sem=recv, device_id=who,
            device_id_type=MESH)

    def enter(self):
        barrier = pltpu.get_barrier_semaphore()
        greeted = [((self.i + k) % 8, self.j) for k in range(1, 8)] + [self.cpart, self.xpart]
        for who in greeted:
            pl.semaphore_signal(barrier, inc=1, device_id=who, device_id_type=MESH)
        pl.semaphore_wait(barrier, len(greeted))

    def var_copy(self, k):
        return self.remote(self.var, self.varies.at[self.i], self.vs.at[k - 1],
                           self.vr.at[self.i], ((self.i + k) % 8, self.j))

    def var_send(self):
        self.varies[self.i] = self.var[...]
        for k in range(1, 8):
            self.var_copy(k).start()

    def var_wait(self):
        for k in range(1, 8):
            n = (self.i + k) % 8
            self.remote(self.var, self.varies.at[n], self.vs.at[k - 1], self.vr.at[n],
                        self.cpart).wait_recv()

    def slot(self, colour):
        return (self.i * 3 + 1 + colour) % 4

    def copy1(self, s):
        theirs = pl.multiple_of((1 - self.core) * 2 * self.quarter, 2 * self.quarter)
        return self.remote(self.part.at[s, pl.ds(theirs, 2 * self.quarter)], self.rec1.at[s],
                           self.s1.at[s], self.r1.at[s], self.cpart)

    def copy2(self, s):
        theirs = pl.multiple_of((1 - self.x) * self.quarter, self.quarter)
        return self.remote(self.acc1.at[s, pl.ds(theirs, self.quarter)], self.rec2.at[s],
                           self.s2.at[s], self.r2.at[s], self.xpart)

    def copy3(self, s):
        n = s // 2
        return self.remote(self.acc2.at[s], self.rec3.at[n], self.s3.at[n], self.r3.at[n],
                           ((self.i + s + 7) % 8, self.j))

    def reduce0(self, colour):
        s = self.slot(colour)

        @pl.when(s < 3)
        def _():
            self.copy1(s).start()

    def reduce1(self, colour):
        s = self.slot(colour)

        @pl.when(s < 3)
        def _():
            self.copy1(s).wait_recv()
            mine = pl.multiple_of(self.core * 2 * self.quarter, 2 * self.quarter)
            self.acc1[s] = self.part[s, pl.ds(mine, 2 * self.quarter)] + self.rec1[s]
            self.copy2(s).start()

    def reduce2(self, colour):
        s = self.slot(colour)

        @pl.when(s < 3)
        def _():
            self.copy2(s).wait_recv()
            mine = pl.multiple_of(self.x * self.quarter, self.quarter)
            self.acc2[s] = self.acc1[s, pl.ds(mine, self.quarter)] + self.rec2[s]

        @pl.when(s % 2 == 0)
        def _():
            self.copy3(s).start()

    def planes(self, colour):
        f = (self.z - colour // 2 + 1) // 3
        return f, 1 - f

    def rows(self, r):
        step = self.quarter // PIECES
        return pl.ds(r * step, step)

    def block(self, colour, h, r):
        return self.blocks.at[colour // 2 + 2 * h, self.core, colour % 2, self.x, self.rows(r)]

    def copy_z(self, colour, h, r, way):
        block = self.block(colour, h, r)
        return self.remote(block, block, self.zs.at[colour, h, r, way], self.zr.at[colour, h, r],
                           ((self.i + (2, 6)[way]) % 8, self.j))

    def copy_y(self, colour, h, r):
        block = self.block(colour, h, r)
        return self.remote(block, block, self.ys.at[colour, h, r], self.yr.at[colour, h, r],
                           self.ypart)

    def copy_x(self, colour, h, r):
        block = self.block(colour, h, r)
        return self.remote(block, block, self.xs.at[colour, h, r], self.xr.at[colour, h, r],
                           self.xpart)

    def copy_core(self, colour, h, r):
        block = self.blocks.at[colour // 2 + 2 * h, self.core, colour % 2, :, self.rows(r)]
        return self.remote(block, block, self.cs.at[colour, h, r], self.cr.at[colour, h, r],
                           self.cpart)

    def spread(self, colour, h, r, wait=False):
        plane = colour // 2 + 2 * h

        @pl.when((plane <= self.z) & (self.z < 3))
        def _():
            up = self.copy_z(colour, h, r, 0)
            up.wait_send() if wait else up.start()

        @pl.when((plane >= self.z) & (self.z > 0))
        def _():
            down = self.copy_z(colour, h, r, 1)
            down.wait_send() if wait else down.start()

        side = self.copy_y(colour, h, r)
        if wait:
            side.wait_send()
        else:
            side.start()
            self.copy_x(colour, h, r).start()

    def own(self, colour):
        s = self.slot(colour)

        @pl.when(s == 1)
        def _():
            for n in range(2):
                self.remote(self.rec3.at[n], self.rec3.at[n], self.s3.at[n], self.r3.at[n],
                            self.cpart).wait_recv()
            self.blocks[self.z, self.core, self.y, self.x] = (
                self.acc2[1] + self.rec3[0] + self.rec3[1])
            for r in range(PIECES):
                self.spread(colour, self.planes(colour)[0], r)

    def near(self, colour):
        h = self.planes(colour)[0]

        @pl.when((self.y == colour % 2) & (self.slot(colour) != 1))
        def _():
            for r in range(PIECES):
                self.copy_z(colour, h, r, 0).wait_recv()
                self.spread(colour, h, r)

    def far(self, colour):
        h = self.planes(colour)[1]

        @pl.when(self.y == colour % 2)
        def _():
            for r in range(PIECES):
                self.copy_z(colour, h, r, 0).wait_recv()
                self.spread(colour, h, r)

    def side(self, colour):
        @pl.when(self.y != colour % 2)
        def _():
            for h in self.planes(colour):
                for r in range(PIECES):
                    self.copy_y(colour, h, r).wait_recv()
                    self.copy_x(colour, h, r).start()

    def cross(self, colour):
        for h in self.planes(colour):
            for r in range(PIECES):
                self.copy_x(colour, h, r).wait_recv()
                self.copy_core(colour, h, r).start()

    def arrive(self, colour):
        for h in self.planes(colour):
            for r in range(PIECES):
                self.copy_core(colour, h, r).wait_recv()

    def leave(self):
        for k in range(1, 8):
            self.var_copy(k).wait_send()
        for colour in range(NCOL):
            s = self.slot(colour)

            @pl.when(s < 3)
            def _():
                self.copy1(s).wait_send()
                self.copy2(s).wait_send()

            @pl.when(s % 2 == 0)
            def _():
                self.copy3(s).wait_send()

            @pl.when(self.y == colour % 2)
            def _():
                for h in self.planes(colour):
                    for r in range(PIECES):
                        self.spread(colour, h, r, wait=True)

            for h in self.planes(colour):
                for r in range(PIECES):
                    self.copy_x(colour, h, r).wait_send()
                    self.copy_core(colour, h, r).wait_send()


def gather_window(part, columns):
    part = lax.psum(part.astype(F32), "gy").astype(BF16)

    def shifted(block, by):
        return lax.ppermute(block, "gx", [((n + by) % columns, n) for n in range(columns)])

    whole = part[1] + shifted(part[0], 1) + shifted(part[2], -1)
    return jnp.stack([whole if n == 4 else shifted(whole, n - 4) for n in range(WINDOW)])


def split(a):
    high = a.astype(BF16)
    return high, (a - high.astype(F32)).astype(BF16)


def prod(a, b):
    ah, al = split(a)
    bh, bl = split(b)
    left = jnp.concatenate([ah, al, ah], axis=1)
    right = jnp.concatenate([bh, bh, bl], axis=0)
    return jnp.dot(left, right, preferred_element_type=F32)


def newton_step(left, right):
    lh, ll = split(left)
    rh, rl = split(right)
    p = jnp.dot(rh, lh, preferred_element_type=F32).astype(BF16)
    left_p = jnp.dot(jnp.concatenate([lh, ll], axis=1), jnp.concatenate([p, p], axis=0),
                     preferred_element_type=F32)
    p_right = jnp.dot(jnp.concatenate([p, p], axis=1), jnp.concatenate([rh, rl], axis=0),
                      preferred_element_type=F32)
    return 1.5 * left - 0.5 * left_p, 1.5 * right - 0.5 * p_right


NT = (((1,), (1,)), ((), ()))


def colours(x_ref, blocks, varies, cf_ref, out_ref, obs_ref, state, proj_ref, tr, trt, lm, rm,
            half, stages=None):
    tile_rows, members = x_ref.shape
    quarter = blocks.shape[4]
    size = 4 * quarter
    eye_mask = lax.broadcasted_iota(jnp.int32, (size, size), 0) == lax.broadcasted_iota(
        jnp.int32, (size, size), 1)
    eye = jnp.where(eye_mask, 1.0, 0.0).astype(F32)

    def newton(rl):
        return 1.5 * eye - 0.5 * rl

    def batch_rows(colour, h):
        return jnp.concatenate(
            [blocks[colour // 2 + 2 * h, core, colour % 2, x] for core in range(2)
             for x in range(2)], axis=0)

    def subtract(ref, scale, left, right):
        for n in range(0, members, CHUNK):
            inc = jnp.dot(left, right(n), preferred_element_type=F32)
            ref[:, n : n + CHUNK] = ref[:, n : n + CHUNK] - scale * inc

    def catch_up(colour, earlier):
        first = tile_rows + 2 * colour * size
        rows = state[...].astype(BF16)
        total = 0.0
        for h in range(2):
            n = 2 * earlier + h
            scale = cf_ref[first : first + 2 * size, n : n + 1]
            proj = jnp.dot(rows, trt[earlier, h], preferred_element_type=F32)
            proj_ref[:, h * size : (h + 1) * size] = jnp.where(scale > 0, proj, 0.0).astype(BF16)
            total = total + scale
        subtract(state, total, proj_ref[...], lambda n: jnp.concatenate(
            [tr[earlier, h, :, n : n + CHUNK] for h in range(2)], axis=0))

    def own_tile(colour):
        offset = (lax.axis_index("gx") + 3 * colour) % NCOL

        @pl.when(offset != 2)
        def _():
            h = half(colour, offset)
            scale = cf_ref[:tile_rows, 2 * colour : 2 * colour + 1] + cf_ref[
                :tile_rows, 2 * colour + 1 : 2 * colour + 2]
            proj = jnp.dot(out_ref[...].astype(BF16), trt[colour, h], preferred_element_type=F32)
            subtract(out_ref, scale, proj.astype(BF16), lambda n: tr[colour, h, :, n : n + CHUNK])

    stage = stages or (lambda colour, at: None)
    if stages is None:
        out_ref[...] = x_ref[...]
    for colour in range(NCOL):
        stage(colour, "start")
        for h in range(2):
            rows = batch_rows(colour, h)
            if colour:
                state[h * size : (h + 1) * size] = rows.astype(F32)
            else:
                obs_ref[h] = rows
        if colour:
            for earlier in range(colour):
                catch_up(colour, earlier)
            for h in range(2):
                obs_ref[h] = state[h * size : (h + 1) * size].astype(BF16)
        stage(colour, "caught")
        traces = []
        for h in range(2):
            obs = obs_ref[h]
            gram = lax.dot_general(obs, obs, NT, preferred_element_type=F32) / (members - 1)
            gram = gram + jnp.where(eye_mask, varies[colour + NCOL * h], 0.0)
            trace = jnp.sum(jnp.where(eye_mask, gram, 0.0))
            traces.append(trace)
            left = gram / trace
            q = newton(left)
            lm[h] = prod(left, q)
            rm[h] = q

        def step(k, carry):
            for at in range(NS_STEPS - 2):
                if stages and stages(colour, at, True):
                    @pl.when(k == at)
                    def _():
                        stages(colour, at)
            for h in range(2):
                lm[h], rm[h] = newton_step(lm[h], rm[h])
            return carry

        lax.fori_loop(0, NS_STEPS - 2, step, 0)
        stage(colour, "rooted")
        for h in range(2):
            right = rm[h]
            right = prod(newton(prod(right, lm[h])), right)
            root = (right / jnp.sqrt(traces[h])).astype(BF16)
            spread = jnp.dot(root, obs_ref[h], preferred_element_type=F32)
            tr[colour, h] = spread.astype(BF16)
            trt[colour, h] = spread.T.astype(BF16)
        stage(colour, "moved")
        own_tile(colour)


def table(*rows):
    return {row[:2]: row[2:] for row in rows}


SCHEDULE = table(
    (0, 0, ("reduce2", 2), ("far", 1)),
    (0, 4, ("side", 1), ("own", 2)),
    (0, 8, ("cross", 1), ("near", 2), ("reduce1", 3)),
    (0, "moved", ("reduce2", 3), ("far", 2)),
    (1, "start", ("arrive", 1),),
    (1, "caught", ("side", 2), ("own", 3)),
    (1, 3, ("near", 3),),
    (1, 5, ("cross", 2),),
    (1, 8, ("far", 3),),
    (2, "start", ("arrive", 2),),
    (2, "caught", ("side", 3),),
    (2, 5, ("cross", 3),),
    (3, "start", ("arrive", 3),),
)


def gathered_kernel(x_ref, part, var, cf_ref, out_ref, blocks, varies, obs_ref, state, proj_ref,
                    tr, trt, lm, rm, rec1, acc1, rec2, acc2, rec3, *sems):
    gather = Gather(part, var, blocks, varies, (rec1, acc1, rec2, acc2, rec3), sems)
    gather.enter()
    for colour in range(NCOL):
        gather.reduce0(colour)
    gather.var_send()
    gather.reduce1(0)
    gather.reduce2(0)
    out_ref[...] = x_ref[...]
    gather.own(0)
    gather.near(0)
    gather.reduce1(1)
    gather.far(0)
    gather.side(0)
    gather.reduce2(1)
    gather.own(1)
    gather.cross(0)
    gather.reduce1(2)
    gather.near(1)
    gather.var_wait()
    gather.arrive(0)

    def stages(colour, at, ask=False):
        todo = SCHEDULE.get((colour, at), ())
        if not ask:
            for name, which in todo:
                getattr(gather, name)(which)
        return bool(todo)

    def half(colour, offset):
        batch = lax.axis_index("gx") + 8 - offset + NCOL * (offset // 3)
        return batch % 8 // NCOL

    colours(x_ref, blocks, varies, cf_ref, out_ref, obs_ref, state, proj_ref, tr, trt, lm, rm,
            half, stages)
    gather.leave()


def window_kernel(*refs):
    colours(*refs, lambda colour, offset: 1 - offset % 3 % 2)


def compute_scratch(size, members):
    return [
        pltpu.VMEM((2, size, members), BF16),
        pltpu.VMEM((2 * size, members), F32),
        pltpu.VMEM((2 * size, 2 * size), BF16),
        pltpu.VMEM((NCOL, 2, size, members), BF16),
        pltpu.VMEM((NCOL, 2, members, size), BF16),
        pltpu.VMEM((2, size, size), F32),
        pltpu.VMEM((2, size, size), F32),
    ]


def gathered_call(tile, part, var, coef):
    size, members = part.shape[1:]
    quarter = size // 4
    vm = lambda *shape: pltpu.VMEM(shape, BF16)
    dma = lambda *shape: pltpu.SemaphoreType.DMA(shape)
    return pl.pallas_call(
        gathered_kernel,
        out_shape=jax.ShapeDtypeStruct(tile.shape, F32),
        in_specs=[pl.BlockSpec(memory_space=pltpu.VMEM)] * 4,
        out_specs=pl.BlockSpec(memory_space=pltpu.VMEM),
        scratch_shapes=[
            vm(4, 2, 2, 2, quarter, members), pltpu.VMEM((8, 1, size), F32),
            *compute_scratch(size, members),
            vm(3, 2 * quarter, members), vm(3, 2 * quarter, members),
            vm(3, quarter, members), vm(3, quarter, members), vm(2, quarter, members),
            dma(3), dma(3), dma(3), dma(3), dma(2), dma(2),
            dma(4, 2, PIECES, 2), *[dma(4, 2, PIECES)] * 7, dma(7), dma(8),
        ],
        compiler_params=pltpu.CompilerParams(
            collective_id=0, has_side_effects=True, vmem_limit_bytes=48 * 2**20),
    )(tile, part, var, coef)


def colours_call(tile, blocks, var, coef):
    size, members = 4 * blocks.shape[4], blocks.shape[5]
    return pl.pallas_call(
        window_kernel,
        out_shape=jax.ShapeDtypeStruct(tile.shape, F32),
        in_specs=[pl.BlockSpec(memory_space=pltpu.VMEM)] * 4,
        out_specs=pl.BlockSpec(memory_space=pltpu.VMEM),
        scratch_shapes=compute_scratch(size, members),
        compiler_params=pltpu.CompilerParams(vmem_limit_bytes=48 * 2**20),
    )(tile, blocks, var, coef)


def on_device(tile, obs_rows, obs_var, taper_level):
    tile_rows, members = tile.shape
    columns, groups = lax.axis_size("gx"), lax.axis_size("gy")
    column, group = lax.axis_index("gx"), lax.axis_index("gy")
    column_rows = groups * tile_rows
    size = obs_rows.shape[1]

    near = (column - 1 + jnp.arange(SLOTS)) % columns
    first = (2 - jnp.arange(SLOTS)) * column_rows + group * tile_rows
    local = (obs_rows[near] - first[:, None]).reshape(-1, 1)
    pick = (local == jnp.arange(tile_rows)[None, :]).astype(BF16)
    part = jnp.dot(pick, tile.astype(BF16), preferred_element_type=F32).astype(BF16)
    part = part.reshape(SLOTS, size, members)

    exact = (columns, groups) == (8, 4)
    if exact:
        batches = jnp.array([b for n in range(NCOL) for b in (n, n + NCOL)], jnp.int32)
        by_colour = lambda a: a.reshape(2, NCOL, -1).transpose(1, 0, 2).reshape(WINDOW, -1)
    else:
        window = gather_window(part, columns)
        base = (column + columns - 4) % columns
        at = (jnp.arange(NCOL) - base) % NCOL
        at = jnp.concatenate([at, at + NCOL])
        batches = (base + at) % columns
        blocks = window[at].reshape(4, 2, 2, 2, size // 4, members).transpose(0, 2, 1, 3, 4, 5)
        var = lax.all_gather(obs_var, "gx", axis=0, tiled=True)[batches][:, None]
        batches = batches.reshape(2, NCOL).T.reshape(-1)
        by_colour = lambda a: a[batches].reshape(WINDOW, -1)

    rows_w = by_colour(obs_rows)
    col_w = ((batches - 1)[:, None] + rows_w // column_rows) % columns
    tile_w = (rows_w % column_rows) // tile_rows
    col_all = jnp.concatenate([jnp.full((tile_rows,), column), col_w.reshape(-1)])
    tile_all = jnp.concatenate([jnp.full((tile_rows,), group), tile_w.reshape(-1)])
    slot = (col_all[:, None] - batches[None, :] + 1) % columns
    spot = jnp.where(slot < SLOTS, slot * groups + tile_all[:, None], -1)
    levels = by_colour(taper_level).astype(F32)
    hit = spot[:, :, None] == jnp.arange(SLOTS * groups)[None, None, :]
    coef = jnp.sum(jnp.where(hit, levels[None], 0.0), axis=-1) / 3.0 / (members - 1)
    if exact:
        return gathered_call(tile, part, obs_var, coef)
    return colours_call(tile, blocks, var, coef)


def solution(mesh):
    in_specs = (P(("gx", "gy"), None), P(), P("gx", None), P())
    out_specs = P(("gx", "gy"), None)
    return jax.shard_map(
        on_device, mesh=mesh, in_specs=in_specs, out_specs=out_specs, check_vma=False
    )
```

profile of v0, /device:TPU:4, one launch (start us, length us, event | category | flops | bytes accessed | tf_op | source)
XLA Modules:
  0.0 128.1 jit_solution(16986651746527764581)
XLA Ops:
  0.0 1.3 gather_fusion
  1.3 0.1 broadcast_subtract_fusion
  1.4 0.7 convert_element_type.25
  2.1 0.1 convert_element_type.26
  2.2 0.1 copy.14
  2.3 0.1 copy.15
  2.4 0.7 broadcast_bitcast_fusion
  3.1 0.7 reshape.151
  3.9 0.8 add_select_fusion.1
  4.6 0.2 select_reduce_fusion
  4.8 0.4 copy.16
  5.2 0.0 copy-start.1
  5.2 0.1 broadcast_multiply_fusion.cf_ref
  5.4 1.5 %copy-done.1 = f32[512,1024]{1,0:T(8,128)S(1)} copy-done((f32[512,1024]{1,0:T(8,128)S(1)}, f32[512,1024]{1,0:T(8,128)}, u32[]{:S(2)}) %copy-start.1) | copy-done | bytes 2097176
  6.8 0.0 copy-start
  6.8 1.0 convolution_convert_fusion
  7.9 0.0 copy-done
  7.9 118.9 %shard_map.55 = f32[512,1024]{1,0:T(8,128)S(1)} custom-call(f32[512,1024]{1,0:T(8,128)} %x_ref.1, bf16[3,256,1024]{2,1,0:T(8,128)(2,1)S(1)} %bitcast.15, f32[1,256]{1,0:T(1,128)S(1)} %copy-done, f32[2560,8]{1,0:T(8,128)S(1)} %broadcast_multiply_fusion.cf_ref), custom_call_target="tpu_custom_call" | custom-call | tf_op jit(solution)/shard_map/pallas_call | solution.py:452
  126.8 1.3 %copy.23 = f32[512,1024]{1,0:T(8,128)} copy(f32[512,1024]{1,0:T(8,128)S(1)} %shard_map.55) | data formatting | bytes 4194304
  (10 shorter events, 0.1 us)
Async XLA Ops:
  5.2 1.6 %copy-start.1 = (f32[512,1024]{1,0:T(8,128)S(1)}, f32[512,1024]{1,0:T(8,128)}, u32[]{:S(2)}) copy-start(f32[512,1024]{1,0:T(8,128)} %x_ref.1) | copy-start | bytes 6291460
  6.8 1.0 copy-start
where the time goes:
time: 128 us
  Pallas kernels  119 us (93%)
  local copies, waits for them, and re-layouts  6.2 us (5%)
  other arithmetic  1.87 us (1%)
    pallas_call x1, Pallas kernels, gathered_call(): pl.pallas_call(gathered_kernel, out_shape=jax.ShapeDtypeStruct(tile.shape...  119 us
    unnamed x8, local copies, waits for them, and re-layouts  3.53 us

commit v1 on v0

--- a/solution.py
+++ b/solution.py
@@ -373,19 +373,20 @@
 
 
 SCHEDULE = table(
-    (0, 0, ("reduce2", 2), ("far", 1)),
-    (0, 4, ("side", 1), ("own", 2)),
-    (0, 8, ("cross", 1), ("near", 2), ("reduce1", 3)),
-    (0, "moved", ("reduce2", 3), ("far", 2)),
-    (1, "start", ("arrive", 1),),
-    (1, "caught", ("side", 2), ("own", 3)),
-    (1, 3, ("near", 3),),
-    (1, 5, ("cross", 2),),
-    (1, 8, ("far", 3),),
-    (2, "start", ("arrive", 2),),
-    (2, "caught", ("side", 3),),
-    (2, 5, ("cross", 3),),
-    (3, "start", ("arrive", 3),),
+    (0, "caught", ("own", 2)),
+    (0, 2, ("side", 1), ("reduce2", 3)),
+    (0, 5, ("near", 2)),
+    (0, 7, ("cross", 1)),
+    (0, "rooted", ("own", 3)),
+    (0, "moved", ("far", 2)),
+    (1, "start", ("arrive", 1)),
+    (1, "caught", ("near", 3), ("side", 2)),
+    (1, 4, ("far", 3)),
+    (1, 6, ("cross", 2)),
+    (2, "start", ("arrive", 2)),
+    (2, "caught", ("side", 3)),
+    (2, 5, ("cross", 3)),
+    (3, "start", ("arrive", 3)),
 )
 
 
@@ -400,15 +401,18 @@
     gather.reduce2(0)
     out_ref[...] = x_ref[...]
     gather.own(0)
+    gather.reduce1(1)
     gather.near(0)
-    gather.reduce1(1)
+    gather.reduce2(1)
     gather.far(0)
+    gather.own(1)
     gather.side(0)
-    gather.reduce2(1)
-    gather.own(1)
-    gather.cross(0)
     gather.reduce1(2)
     gather.near(1)
+    gather.cross(0)
+    gather.reduce2(2)
+    gather.far(1)
+    gather.reduce1(3)
     gather.var_wait()
     gather.arrive(0)
 

time: 128 us -> 125 us (0.977)
  Pallas kernels: 119 us -> 115 us
    pallas_call x1, Pallas kernels: 119 us -> 115 us  [gathered_call(): pl.pallas_call(gathered_kernel, out_shape=jax.ShapeDtypeStruct(tile.shape...]
where the time goes in v1:
time: 125 us; the launch traced here: 124 us
  Pallas kernels  115 us (92%)
  local copies, waits for them, and re-layouts  6.2 us (5%)
  other arithmetic  1.87 us (1%)
    pallas_call x1, Pallas kernels, gathered_call(): pl.pallas_call(gathered_kernel, out_shape=jax.ShapeDtypeStruct(tile.shape...  115 us
    unnamed x8, local copies, waits for them, and re-layouts  3.53 us

profile of v1, /device:TPU:4, one launch (start us, length us, event | category | flops | bytes accessed | tf_op | source)
XLA Modules:
  0.0 124.5 jit_solution(974550677232995212)
XLA Ops:
  0.0 1.3 %gather_fusion = s32[3,256]{1,0:T(4,128)S(1)} fusion(s32[8,256]{1,0:T(8,128)} %param.6, s32[1024]{0:T(1024)S(1)} %pad_clamp_fusion), kind=kCustom, calls=%fused_computation | custom fusion | bytes 6156 | tf_op jit(solution)/shard_map/gather | solution.py:495
  1.3 0.1 broadcast_subtract_fusion
  1.4 0.7 convert_element_type.25
  2.1 0.1 convert_element_type.26
  2.2 0.1 copy.14
  2.3 0.1 copy.15
  2.4 0.7 broadcast_bitcast_fusion
  3.1 0.7 reshape.151
  3.9 0.8 add_select_fusion.1
  4.6 0.2 select_reduce_fusion
  4.8 0.4 copy.16
  5.2 0.0 copy-start.1
  5.2 0.1 broadcast_multiply_fusion.cf_ref
  5.4 1.5 %copy-done.1 = f32[512,1024]{1,0:T(8,128)S(1)} copy-done((f32[512,1024]{1,0:T(8,128)S(1)}, f32[512,1024]{1,0:T(8,128)}, u32[]{:S(2)}) %copy-start.1) | copy-done | bytes 2097176
  6.8 0.0 copy-start
  6.8 1.0 convolution_convert_fusion
  7.9 0.0 copy-done
  7.9 115.3 %shard_map.55 = f32[512,1024]{1,0:T(8,128)S(1)} custom-call(f32[512,1024]{1,0:T(8,128)} %x_ref.1, bf16[3,256,1024]{2,1,0:T(8,128)(2,1)S(1)} %bitcast.15, f32[1,256]{1,0:T(1,128)S(1)} %copy-done, f32[2560,8]{1,0:T(8,128)S(1)} %broadcast_multiply_fusion.cf_ref), custom_call_target="tpu_custom_call" | custom-call | tf_op jit(solution)/shard_map/pallas_call | solution.py:456
  123.2 1.3 %copy.23 = f32[512,1024]{1,0:T(8,128)} copy(f32[512,1024]{1,0:T(8,128)S(1)} %shard_map.55) | data formatting | bytes 4194304
  (10 shorter events, 0.1 us)
Async XLA Ops:
  5.2 1.6 %copy-start.1 = (f32[512,1024]{1,0:T(8,128)S(1)}, f32[512,1024]{1,0:T(8,128)}, u32[]{:S(2)}) copy-start(f32[512,1024]{1,0:T(8,128)} %x_ref.1) | copy-start | bytes 6291460
  6.8 1.0 copy-start
